TPU v7x, 32 devices: a whole 2x2x4 slice. The times are simulated.
32 devices in a mesh: seq: 8 (over y, x, core), tp: 4 (over z).
Axes of the slice: x: 2, y: 2, z: 4, core: 2. Of those that a mesh axis runs over, the one named last changes fastest.
Arguments:
- codes: bfloat16 [4096, 4096], P('seq', 'tp'), may hold values from -127 to 127, as said below
- exponents: int32 [4096], P('seq'), may hold values from -8 to -5
- w_query: bfloat16 [4096, 4096], P(None, 'tp'), may hold values from -0.09375 to 0.09375
- w_key: bfloat16 [4096, 4096], P(None, 'tp'), may hold values from -0.09375 to 0.09375
- w_value: bfloat16 [4096, 4096], P(None, 'tp'), may hold values from -0.09375 to 0.09375
- norm_gain: float32 [4096], P('tp'), may hold values from 0.1 to 1.9
- w_out: bfloat16 [4096, 4096], P('tp'), may hold values from -0.09375 to 0.09375
Outputs:
- mixed: bfloat16 [4096, 4096], P(('seq', 'tp'))
Inputs may be any that keep to these rules, and one draw needn't show every extreme that they name: `codes`: every entry is a whole number.
All inputs are finite; a program needn't handle non-finite values.
Results may differ from a plain program's by a relative error of at most 0.012.
Values may be sent and summed in bfloat16 or wider, within the bound.
A program may use at most 128 MiB of HBM per device.

v0:
```python
import jax
import jax.numpy as jnp
from jax import lax
from jax.sharding import PartitionSpec as P

HD = 128
BLK = 512


def on_device(codes, exponents, w_query, w_key, w_value, norm_gain, w_out):
    tok_count = codes.shape[0]
    local_width = w_query.shape[1]
    heads_local = local_width // HD
    blocks = tok_count // BLK
    row_scale = jnp.exp2(exponents.astype(jnp.float32))[:, None]
    weights = (w_query, w_key, w_value)
    piece = lax.all_gather(codes, "tp", axis=1, tiled=True)
    query, keys, values = tuple(
        (jnp.dot(piece, weight, preferred_element_type=jnp.float32) for weight in weights)
    )
    feat_q = (
        (jax.nn.elu(query * row_scale) + 1.0)
        .astype(jnp.bfloat16)
        .reshape(blocks, BLK, heads_local, HD)
    )
    feat_k = (
        (jax.nn.elu(keys * row_scale) + 1.0)
        .astype(jnp.bfloat16)
        .reshape(blocks, BLK, heads_local, HD)
    )
    value_b = (values * row_scale).astype(jnp.bfloat16).reshape(blocks, BLK, heads_local, HD)
    block_states = jnp.einsum(
        "bshd,bshe->bhde", feat_k, value_b, preferred_element_type=jnp.float32
    )
    shard_state = jnp.sum(block_states, axis=0)
    my_index = lax.axis_index("seq")
    piece = lax.all_gather(shard_state[None], "seq", axis=0, tiled=True)
    owners = jnp.arange(piece.shape[0], dtype=jnp.int32)
    keep = (owners < my_index).astype(jnp.float32)
    before = jnp.sum(piece * keep[:, None, None, None], axis=0)
    states = (before[None] + (jnp.cumsum(block_states, axis=0) - block_states)).astype(jnp.bfloat16)
    inter = jnp.einsum("bshd,bhde->bshe", feat_q, states, preferred_element_type=jnp.float32)
    causal = jnp.tril(jnp.ones((BLK, BLK), jnp.float32))
    scores = jnp.einsum("bshd,bthd->bhst", feat_q, feat_k, preferred_element_type=jnp.float32)
    scores = (scores * causal[None, None]).astype(jnp.bfloat16)
    intra = jnp.einsum("bhst,bthe->bshe", scores, value_b, preferred_element_type=jnp.float32)
    summed = inter + intra
    mean_sq = jnp.mean(summed * summed, axis=-1, keepdims=True)
    gain = norm_gain.reshape(heads_local, HD)
    normed = (
        (summed * lax.rsqrt(mean_sq + 1e-05) * gain)
        .astype(jnp.bfloat16)
        .reshape(tok_count, local_width)
    )
    return lax.psum_scatter(
        jnp.dot(normed, w_out, preferred_element_type=jnp.float32).astype(jnp.bfloat16),
        "tp",
        scatter_dimension=0,
        tiled=True,
    )


def solution(mesh):
    in_specs = (
        P("seq", "tp"),
        P("seq"),
        P(None, "tp"),
        P(None, "tp"),
        P(None, "tp"),
        P("tp"),
        P("tp", None),
    )
    out_specs = P(("seq", "tp"), None)
    return jax.shard_map(
        on_device, mesh=mesh, in_specs=in_specs, out_specs=out_specs, check_vma=False
    )
```

profile of v0, /device:TPU:12, one launch (start us, length us, event | category | flops | bytes accessed | tf_op | source)
XLA Modules:
  0.0 253.2 jit_solution(7981739408371218121)
XLA Ops:
  6.5 0.0 all-gather.4.cloned.1.call-start
  6.5 0.7 all-gather.4.cloned.1.call-update
  7.3 0.0 all-gather.6.cloned.1.call-start
  7.3 0.7 multiply_exponential_fusion
  8.0 80.4 %all-gather.4.cloned.1.call-done = bf16[512,4096]{1,0:T(8,128)(2,1)} async-done(((bf16[512,1024]{1,0:T(8,128)(2,1)}), bf16[512,4096]{1,0:T(8,128)(2,1)}) %all-gather.4.cloned.1.call-update) | async-done | bytes 4194320 | tf_op jit(solution)/shard_map/all_gather | solution.py:17
  88.4 9.8 %fusion.6 = bf16[512,1024]{1,0:T(8,128)(2,1)S(1)} fusion(bf16[512,4096]{1,0:T(8,128)(2,1)} %all-gather.4.cloned.1.call-done, bf16[4096,1024]{1,0:T(8,128)(2,1)} %param.10, f32[512]{0:T(512)S(1)} %multiply_exponential_fusion), kind=kOutput, calls=%fused_computation.12 | convolution fusion | flops 4298113024 | bytes 13633536 | tf_op jit(solution)/shard_map/dot_general | solution.py:19
  98.2 0.5 copy.19
  98.8 9.1 %multiply_convert_fusion.2 = bf16[512,1024]{1,0:T(8,128)(2,1)S(1)} fusion(bf16[512,4096]{1,0:T(8,128)(2,1)} %all-gather.4.cloned.1.call-done, bf16[4096,1024]{1,0:T(8,128)(2,1)} %param.11, f32[512]{0:T(512)S(1)} %multiply_exponential_fusion), kind=kOutput, calls=%fused_computation.21 | convolution fusion | flops 4296015872 | bytes 13633536 | tf_op jit(solution)/shard_map/dot_general | solution.py:19
  107.9 0.5 copy.20
  108.5 1.2 fusion.25
  109.7 0.0 all-gather.6.cloned.1.call-update
  109.7 0.2 reduce-scatter.2.cloned.1.call-start
  110.0 1.2 fusion.19
  111.1 10.8 %fusion.14 = bf16[64,8,8,128]{3,2,1,0:T(8,128)(2,1)} fusion(bf16[512,4096]{1,0:T(8,128)(2,1)} %all-gather.4.cloned.1.call-done, bf16[4096,1024]{1,0:T(8,128)(2,1)} %param.9, f32[512]{0:T(512)S(1)} %multiply_exponential_fusion), kind=kOutput, calls=%fused_computation.23 | convolution fusion | flops 4298113024 | bytes 13633536 | tf_op jit(solution)/shard_map/dot_general | solution.py:19
  121.9 0.0 copy-start
  121.9 25.5 %all-gather.6.cloned.1.call-done = f32[64,128,128]{2,1,0:T(8,128)} async-done(((f32[8,128,128]{2,1,0:T(8,128)}), f32[64,128,128]{2,1,0:T(8,128)}) %all-gather.6.cloned.1.call-update) | async-done | bytes 4194320 | tf_op jit(solution)/shard_map/all_gather | solution.py:37
  147.4 0.0 copy-start.1
  147.4 2.8 %multiply_reduce_fusion = f32[8,128,128]{2,1,0:T(8,128)S(1)} fusion(f32[8,8,128,128]{3,2,1,0:T(8,128)} %bitcast.42, f32[8]{0:T(128)S(1)} %compare_convert_fusion), kind=kLoop, calls=%fused_computation.8 | loop fusion | flops 1966080 | bytes 4718624 | tf_op jit(solution)/shard_map/reduce_sum | solution.py:40
  150.3 0.0 copy-done
  150.3 0.0 copy-done.1
  150.3 1.8 fusion.17
  152.1 0.0 copy-start.2
  152.1 6.1 %fusion.10 = (f32[512,8]{0,1:T(8,128)S(1)}, f32[8,128,512]{2,1,0:T(8,128)}) fusion(f32[8,128,512]{2,1,0:T(8,128)} %fusion.17, bf16[512,8,128]{0,2,1:T(8,128)(2,1)S(1)} %bitcast.41, f32[512,512]{1,0:T(8,128)} %fusion.19, bf16[512,8,128]{0,2,1:T(8,128)(2,1)S(1)} %bitcast.39, bf16[64,8,8,128]{3,2,1,0:T(8,128)(2,1)} %fusion.14), kind=kOutput, calls=%fused_computation.18 | convolution fusion | flops 1079504896 | bytes 8404992 | tf_op jit(solution)/shard_map/bhst,bthe->bshe/dot_general | solution.py:46
  158.2 0.0 copy-done.2
  158.2 1.9 fusion.12
  160.1 9.5 %convolution_convert_fusion = bf16[512,4096]{1,0:T(8,128)(2,1)} fusion(bf16[512,1024]{0,1:T(8,128)(2,1)S(1)} %bitcast.43, bf16[1024,4096]{1,0:T(8,128)(2,1)} %param.13), kind=kOutput, calls=%fused_computation.5 | convolution fusion | flops 4297064448 | bytes 13631488 | tf_op jit(solution)/shard_map/dot_general | solution.py:56
  169.6 0.0 reduce-scatter.2.cloned.1.call-update
  169.6 77.1 %reduce-scatter.2.cloned.1.call-done = bf16[128,4096]{1,0:T(8,128)(2,1)} async-done(((bf16[512,4096]{1,0:T(8,128)(2,1)}), bf16[128,4096]{1,0:T(8,128)(2,1)}) %reduce-scatter.2.cloned.1.call-update) | async-done | bytes 1048592 | tf_op jit(solution)/shard_map/reduce_scatter | solution.py:55
  (2 shorter events, 0.0 us)
Async XLA Ops:
  6.5 81.9 %all-gather.4.cloned.1.call-start = ((), (), s32[]{:S(2)}) async-start(), calls=%async_computation.1 | async-start | bytes 5242880 | tf_op jit(solution)/shard_map/all_gather | solution.py:17
  7.3 140.2 %all-gather.6.cloned.1.call-start = ((), (), s32[]{:S(2)}) async-start(), calls=%async_computation.3 | async-start | bytes 4718592 | tf_op jit(solution)/shard_map/all_gather | solution.py:37
  109.7 137.0 %reduce-scatter.2.cloned.1.call-start = ((), (), s32[]{:S(2)}) async-start(), calls=%async_computation.2 | async-start | bytes 5242880 | tf_op jit(solution)/shard_map/reduce_scatter | solution.py:55
  121.9 28.3 %copy-start = (f32[8,128,128]{2,1,0:T(8,128)S(1)}, f32[8,128,128]{2,1,0:T(8,128)}, u32[]{:S(2)}) copy-start(f32[8,128,128]{2,1,0:T(8,128)} %fusion.25) | copy-start | bytes 1572868
  147.4 2.9 %copy-start.1 = (bf16[64,8,8,128]{3,2,1,0:T(8,128)(2,1)S(1)}, bf16[64,8,8,128]{3,2,1,0:T(8,128)(2,1)}, u32[]{:S(2)}) copy-start(bf16[64,8,8,128]{3,2,1,0:T(8,128)(2,1)} %fusion.14) | copy-start | bytes 3145732
  152.1 6.1 %copy-start.2 = (f32[1024]{0:T(1024)S(1)}, f32[1024]{0:T(1024)}, u32[]{:S(2)}) copy-start(f32[1024]{0:T(1024)} %param.12) | copy-start | bytes 12292
Sparse Core Ops, SparseCore 0:
  8.9 79.4 all-gather.3
  109.8 37.5 all-gather.5
  169.8 76.8 reduce-scatter.1
where the time goes:
time: 255 us; the launch traced here: 253 us
  waiting for transfers between devices  184 us (72%)
  matrix products  48.4 us (19%)
  between operations  13.2 us (5%)
  other arithmetic  6.59 us (3%)
    all_gather x1, waiting for transfers between devices, on_device(): piece = lax.all_gather(codes, 'tp', axis=1, tiled=True)  80.4 us
    reduce_scatter x1, waiting for transfers between devices, on_device(): lax.psum_scatter(jnp.dot(normed, w_out, preferred_element_type=jnp.float3...  77.1 us
    dot_general x3, matrix products, on_device(): jnp.dot(piece, weight, preferred_element_type=jnp.float32)  29.8 us
    all_gather x1, waiting for transfers between devices, on_device(): piece = lax.all_gather(shard_state[None], 'seq', axis=0, tiled=True)  25.5 us
    dot_general x1, matrix products, on_device(): jnp.dot(normed, w_out, preferred_element_type=jnp.float32)  9.5 us
    dot_general x1, matrix products, on_device(): jnp.einsum('bhst,bthe->bshe', scores, value_b, preferred_element_type=jnp...  6.11 us
  transfers between devices with their start and end apart: 3, of which 3 were waited for; matrix products, arithmetic and copies ran while one was open for 5% of the time, Pallas kernels for 0%

commit v1 on v0

v1 whole, which is shorter than its diff:
```python
import functools

import jax
import jax.numpy as jnp
from jax import lax
from jax.experimental import pallas as pl
from jax.experimental.pallas import tpu as pltpu
from jax.sharding import PartitionSpec as P

HD = 128
MESH = pl.DeviceIdType.MESH
GATHER_CHUNKS = 4
OUT_CHUNKS = 8
BF = jnp.bfloat16
F32 = jnp.float32


def feature(t):
    return jnp.where(t > 0, t + 1.0, jnp.exp(jnp.minimum(t, 0.0)))


def kernel(
    n, seqs, x_ref, wq_ref, wk_ref, wv_ref, gain_ref, wo_ref, out_ref,
    xg, w, wo, acc, tot, pre, sbuf, rbuf, part, land,
    x_sem, w_sem, wo_sem, g_send, g_recv, s_send, s_recv, r_send, r_recv,
):
    z = lax.axis_index("tp")
    s = lax.axis_index("seq")
    toks, feats = xg.shape[1], xg.shape[2]
    width = acc.shape[2]
    heads = width // HD
    rows = toks // n
    ow = part.shape[2]
    outs = part.shape[0]
    crows = toks // GATHER_CHUNKS
    steps = seqs.bit_length() - 1

    def partner(i):
        d = 1 << i
        return s + d * (1 - 2 * ((s // d) % 2))

    own = pltpu.make_async_copy(x_ref, xg.at[z], x_sem)
    own.start()

    def w_copy(m, b):
        src = (wq_ref, wk_ref, wv_ref)[m]
        block = pl.ds(pl.multiple_of(b * feats, feats), feats)
        return pltpu.make_async_copy(src.at[block], w.at[m, block], w_sem.at[m, b])

    def each_block(t, fn):
        if t == 0:
            fn(z)
            return
        pl.when(z - t >= 0)(lambda: fn(z - t))
        pl.when(z + t < n)(lambda: fn(z + t))

    def start_w(b):
        for m in range(3):
            w_copy(m, b).start()

    start_w(z)

    barrier = pltpu.get_barrier_semaphore()
    for i in range(steps):
        pl.semaphore_signal(barrier, inc=1, device_id={"seq": partner(i)}, device_id_type=MESH)

    @pl.when(z > 0)
    def _():
        pl.semaphore_signal(barrier, inc=1, device_id={"tp": z - 1}, device_id_type=MESH)

    @pl.when(z < n - 1)
    def _():
        pl.semaphore_signal(barrier, inc=1, device_id={"tp": z + 1}, device_id_type=MESH)

    near = jnp.where(z > 0, 1, 0) + jnp.where(z < n - 1, 1, 0)
    pl.semaphore_wait(barrier, near + steps)

    def g_copy(b, c, up):
        chunk = xg.at[b, pl.ds(c * crows, crows)]
        return pltpu.make_async_remote_copy(
            src_ref=chunk, dst_ref=chunk,
            send_sem=g_send.at[0 if up else 1, b, c], recv_sem=g_recv.at[b, c],
            device_id={"tp": z + 1 if up else z - 1}, device_id_type=MESH,
        )

    def pass_on(b, c, up):
        if up:
            pl.when(z < n - 1)(lambda: g_copy(b, c, True).start())
        else:
            pl.when(z > 0)(lambda: g_copy(b, c, False).start())

    own.wait()
    for c in range(GATHER_CHUNKS):
        pass_on(z, c, True)
        pass_on(z, c, False)

    for t in range(1, n):
        each_block(t, start_w)
    wo_copy = pltpu.make_async_copy(wo_ref, wo, wo_sem)
    wo_copy.start()

    tile = min(256, width)

    def project(b, m, first):
        w_copy(m, b).wait()
        block = pl.ds(pl.multiple_of(b * feats, feats), feats)

        @pl.loop(0, width // tile)
        def _(j):
            cols = pl.ds(pl.multiple_of(j * tile, tile), tile)
            term = jnp.dot(xg[b], w[m, block, cols], preferred_element_type=F32)
            if first:
                acc[m, :, cols] = term
            else:
                acc[m, :, cols] += term

    def project_all(first):
        def go(b):
            for m in (1, 2, 0):
                project(b, m, first)
        return go

    project_all(True)(z)
    for t in range(1, n):
        for c in range(GATHER_CHUNKS):
            @pl.when(z - t >= 0)
            def _():
                g_copy(z - t, c, True).wait_recv()
                pass_on(z - t, c, True)

            @pl.when(z + t < n)
            def _():
                g_copy(z + t, c, False).wait_recv()
                pass_on(z + t, c, False)
        each_block(t, project_all(False))

    for t in range(n):
        for c in range(GATHER_CHUNKS):
            @pl.when((z - t >= 0) & (z < n - 1))
            def _():
                g_copy(z - t, c, True).wait_send()

            @pl.when((z + t < n) & (z > 0))
            def _():
                g_copy(z + t, c, False).wait_send()

    fk, vb, fq, o = xg.at[0], xg.at[1], xg.at[2], xg.at[3]

    def head(h):
        return pl.ds(pl.multiple_of(h * HD, HD), HD)

    @pl.loop(0, heads)
    def _(h):
        cols = head(h)
        key = feature(acc[1, :, cols]).astype(BF)
        val = acc[2, :, cols].astype(BF)
        fk[:, cols] = key
        vb[:, cols] = val
        tot[cols, :] = lax.dot_general(key, val, (((0,), (0,)), ((), ())), preferred_element_type=F32)

    pre[...] = jnp.zeros_like(pre)
    at_or_before = lax.broadcasted_iota(jnp.int32, (toks, toks), 0) >= lax.broadcasted_iota(
        jnp.int32, (toks, toks), 1
    )

    def intra(h):
        cols = head(h)
        qry = feature(acc[0, :, cols]).astype(BF)
        fq[:, cols] = qry
        scores = lax.dot_general(qry, fk[:, cols], (((1,), (1,)), ((), ())), preferred_element_type=F32)
        scores = jnp.where(at_or_before, scores, 0.0).astype(BF)
        acc[0, :, cols] = jnp.dot(scores, vb[:, cols], preferred_element_type=F32)

    def s_copy(i):
        return pltpu.make_async_remote_copy(
            src_ref=sbuf.at[i], dst_ref=rbuf.at[i], send_sem=s_send.at[i], recv_sem=s_recv.at[i],
            device_id={"seq": partner(i)}, device_id_type=MESH,
        )

    for i in range(steps):
        sbuf[i] = tot[...].astype(BF)
        s_copy(i).start()
        pl.loop(i * heads // steps, (i + 1) * heads // steps)(intra)
        s_copy(i).wait()
        came = rbuf[i].astype(F32)
        tot[...] += came

        @pl.when((s // (1 << i)) % 2 == 1)
        def _():
            pre[...] += came

    @pl.loop(0, heads)
    def _(h):
        cols = head(h)
        y = acc[0, :, cols] + jnp.dot(fq[:, cols], pre[cols, :].astype(BF), preferred_element_type=F32)
        mean_sq = jnp.mean(y * y, axis=-1, keepdims=True)
        o[:, cols] = (y * lax.rsqrt(mean_sq + 1e-05) * gain_ref[:, cols]).astype(BF)

    wo_copy.wait()

    def r_copy(c, j, up):
        src = part.at[c, pl.ds(j * rows, rows)]
        slot = j if up else jnp.where(z - 1 == j, n, j)
        return pltpu.make_async_remote_copy(
            src_ref=src, dst_ref=land.at[slot, c],
            send_sem=r_send.at[j, c], recv_sem=r_recv.at[slot, c],
            device_id={"tp": z + 1 if up else z - 1}, device_id_type=MESH,
        )

    def arrived(c, slot):
        ref = land.at[slot, c]
        pltpu.make_async_copy(ref, ref, r_recv.at[slot, c]).wait()
        return land[slot, c].astype(F32)

    def add_landed(c, j):
        mine = pl.ds(j * rows, rows)
        part[c, mine, :] = (part[c, mine, :].astype(F32) + arrived(c, j)).astype(BF)

    @pl.loop(0, outs)
    def _(c):
        cols = pl.ds(pl.multiple_of(c * ow, ow), ow)
        part[c] = jnp.dot(o[...], wo[:, cols], preferred_element_type=F32).astype(BF)
        for k in range(n - 1):
            up_j, down_j = n - 1 - k, k

            @pl.when(z < up_j)
            def _():
                pl.when(z > 0)(lambda: add_landed(c, up_j))
                r_copy(c, up_j, True).start()

            @pl.when(z > down_j)
            def _():
                pl.when(z < n - 1)(lambda: add_landed(c, down_j))
                r_copy(c, down_j, False).start()

    @pl.loop(0, outs)
    def _(c):
        cols = pl.ds(pl.multiple_of(c * ow, ow), ow)
        mine = pl.ds(pl.multiple_of(z * rows, rows), rows)
        total = part[c, mine, :].astype(F32)

        @pl.when(z == 0)
        def _():
            out_ref[:, cols] = (total + arrived(c, n)).astype(BF)

        @pl.when(z == n - 1)
        def _():
            out_ref[:, cols] = (total + arrived(c, n - 1)).astype(BF)

        @pl.when((z > 0) & (z < n - 1))
        def _():
            out_ref[:, cols] = (total + arrived(c, z) + arrived(c, n)).astype(BF)

    @pl.loop(0, outs)
    def _(c):
        for j in range(n):
            pl.when(z < j)(lambda: r_copy(c, j, True).wait_send())
            pl.when(z > j)(lambda: r_copy(c, j, False).wait_send())


def on_device(n, seqs, codes, exponents, w_query, w_key, w_value, norm_gain, w_out):
    toks, feats = codes.shape
    depth, width = w_query.shape
    model = w_out.shape[1]
    rows = toks // n
    ow = model // OUT_CHUNKS
    steps = seqs.bit_length() - 1
    x = (codes.astype(F32) * jnp.exp2(exponents.astype(F32))[:, None]).astype(BF)
    hbm = pl.BlockSpec(memory_space=pl.ANY)
    vmem = pl.BlockSpec(memory_space=pltpu.VMEM)
    dma = pltpu.SemaphoreType.DMA
    return pl.pallas_call(
        functools.partial(kernel, n, seqs),
        out_shape=jax.ShapeDtypeStruct((rows, model), BF),
        in_specs=[hbm, hbm, hbm, hbm, vmem, hbm],
        out_specs=vmem,
        scratch_shapes=[
            pltpu.VMEM((n, toks, feats), BF),
            pltpu.VMEM((3, depth, width), BF),
            pltpu.VMEM((width, model), BF),
            pltpu.VMEM((3, toks, width), F32),
            pltpu.VMEM((width, HD), F32),
            pltpu.VMEM((width, HD), F32),
            pltpu.VMEM((steps, width, HD), BF),
            pltpu.VMEM((steps, width, HD), BF),
            pltpu.VMEM((OUT_CHUNKS, toks, ow), BF),
            pltpu.VMEM((n + 1, OUT_CHUNKS, rows, ow), BF),
            dma(()),
            dma((3, n)),
            dma(()),
            dma((2, n, GATHER_CHUNKS)),
            dma((n, GATHER_CHUNKS)),
            dma((steps,)),
            dma((steps,)),
            dma((n, OUT_CHUNKS)),
            dma((n + 1, OUT_CHUNKS)),
        ],
        compiler_params=pltpu.CompilerParams(
            collective_id=0, has_side_effects=True, vmem_limit_bytes=62 * 1024 * 1024
        ),
        cost_estimate=pl.CostEstimate(
            flops=2 * toks * width * (3 * depth + model) + 4 * toks * toks * width,
            bytes_accessed=2 * (3 * depth * width + width * model),
            transcendentals=2 * toks * width,
        ),
    )(x, w_query, w_key, w_value, norm_gain.reshape(1, width), w_out)


def solution(mesh):
    in_specs = (
        P("seq", "tp"), P("seq"), P(None, "tp"), P(None, "tp"), P(None, "tp"), P("tp"), P("tp", None),
    )
    body = functools.partial(on_device, mesh.shape["tp"], mesh.shape["seq"])
    return jax.shard_map(
        body, mesh=mesh, in_specs=in_specs, out_specs=P(("seq", "tp"), None), check_vma=False
    )
```

time: 255 us -> 197 us (0.77)
  the two profiles are of different devices: /device:TPU:12 before, /device:TPU:0 now
where the time goes in v1:
time: 197 us
  Pallas kernels  192 us (97%)
  other arithmetic  3.12 us (2%)
  local copies, waits for them, and re-layouts  2.29 us (1%)
    pallas_call x1, Pallas kernels, on_device(): pl.pallas_call(functools.partial(kernel, n, seqs), out_shape=jax.ShapeDty...  192 us

profile of v1, /device:TPU:0, one launch (start us, length us, event | category | flops | bytes accessed | tf_op | source)
XLA Modules:
  0.0 197.0 jit_solution(17091968950049126803)
XLA Ops:
  0.0 0.7 multiply_exponential_fusion
  0.7 2.4 %multiply_convert_fusion.x_ref = bf16[512,1024]{1,0:T(8,128)(2,1)} fusion(bf16[512,1024]{1,0:T(8,128)(2,1)} %param.7, f32[512]{0:T(512)S(1)} %multiply_exponential_fusion), kind=kLoop, calls=%fused_computation | loop fusion | flops 1572864 | bytes 2099200 | tf_op jit(solution)/shard_map/convert_element_type | solution.py:268
  3.1 191.6 %shard_map.73 = bf16[128,4096]{1,0:T(8,128)(2,1)} custom-call(bf16[512,1024]{1,0:T(8,128)(2,1)} %multiply_convert_fusion.x_ref, bf16[4096,1024]{1,0:T(8,128)(2,1)} %wq_ref.1, bf16[4096,1024]{1,0:T(8,128)(2,1)} %wk_ref.1, bf16[4096,1024]{1,0:T(8,128)(2,1)} %wv_ref.1, f32[1,1024]{1,0:T(1,128)} %bitcast.1, bf16[1024,4096]{1,0:T(8,128)(2,1)} %wo_ref.1), custom_call_target="tpu_custom_call" | custom-call | flops 18253611008 | bytes 33554432 | tf_op jit(solution)/shard_map/pallas_call | solution.py:272
  194.7 2.3 %copy.9 = bf16[128,4096]{1,0:T(8,128)(2,1)} copy(bf16[128,4096]{1,0:T(8,128)(2,1)} %shard_map.73) | data formatting | bytes 2097152

commit v2 on v1

--- a/solution.py
+++ b/solution.py
@@ -11,6 +11,7 @@
 MESH = pl.DeviceIdType.MESH
 GATHER_CHUNKS = 4
 OUT_CHUNKS = 8
+WINDOW = 2
 BF = jnp.bfloat16
 F32 = jnp.float32
 
@@ -20,8 +21,8 @@
 
 
 def kernel(
-    n, seqs, x_ref, wq_ref, wk_ref, wv_ref, gain_ref, wo_ref, out_ref,
-    xg, w, wo, acc, tot, pre, sbuf, rbuf, part, land,
+    n, seqs, x_ref, exp_ref, wq_ref, wk_ref, wv_ref, gain_ref, wo_ref, out_ref,
+    xg, w, wo, acc, scale, tot, pre, sbuf, rbuf, part, land,
     x_sem, w_sem, wo_sem, g_send, g_recv, s_send, s_recv, r_send, r_recv,
 ):
     z = lax.axis_index("tp")
@@ -99,6 +100,12 @@
     wo_copy = pltpu.make_async_copy(wo_ref, wo, wo_sem)
     wo_copy.start()
 
+    on_diagonal = lax.broadcasted_iota(jnp.int32, (toks, toks), 0) == lax.broadcasted_iota(
+        jnp.int32, (toks, toks), 1
+    )
+    row_scale = jnp.where(on_diagonal, jnp.exp2(exp_ref[...].astype(F32)), 0.0)
+    scale[...] = jnp.broadcast_to(jnp.sum(row_scale, axis=1, keepdims=True), scale.shape)
+
     tile = min(256, width)
 
     def project(b, m, first):
@@ -152,8 +159,8 @@
     @pl.loop(0, heads)
     def _(h):
         cols = head(h)
-        key = feature(acc[1, :, cols]).astype(BF)
-        val = acc[2, :, cols].astype(BF)
+        key = feature(acc[1, :, cols] * scale[...]).astype(BF)
+        val = (acc[2, :, cols] * scale[...]).astype(BF)
         fk[:, cols] = key
         vb[:, cols] = val
         tot[cols, :] = lax.dot_general(key, val, (((0,), (0,)), ((), ())), preferred_element_type=F32)
@@ -165,7 +172,7 @@
 
     def intra(h):
         cols = head(h)
-        qry = feature(acc[0, :, cols]).astype(BF)
+        qry = feature(acc[0, :, cols] * scale[...]).astype(BF)
         fq[:, cols] = qry
         scores = lax.dot_general(qry, fk[:, cols], (((1,), (1,)), ((), ())), preferred_element_type=F32)
         scores = jnp.where(at_or_before, scores, 0.0).astype(BF)
@@ -216,10 +223,16 @@
         mine = pl.ds(j * rows, rows)
         part[c, mine, :] = (part[c, mine, :].astype(F32) + arrived(c, j)).astype(BF)
 
+    def sent(c):
+        for j in range(n):
+            pl.when(z < j)(lambda: r_copy(c, j, True).wait_send())
+            pl.when(z > j)(lambda: r_copy(c, j, False).wait_send())
+
     @pl.loop(0, outs)
     def _(c):
         cols = pl.ds(pl.multiple_of(c * ow, ow), ow)
         part[c] = jnp.dot(o[...], wo[:, cols], preferred_element_type=F32).astype(BF)
+        pl.when(c >= WINDOW)(lambda: sent(c - WINDOW))
         for k in range(n - 1):
             up_j, down_j = n - 1 - k, k
 
@@ -251,11 +264,7 @@
         def _():
             out_ref[:, cols] = (total + arrived(c, z) + arrived(c, n)).astype(BF)
 
-    @pl.loop(0, outs)
-    def _(c):
-        for j in range(n):
-            pl.when(z < j)(lambda: r_copy(c, j, True).wait_send())
-            pl.when(z > j)(lambda: r_copy(c, j, False).wait_send())
+    pl.loop(outs - WINDOW, outs)(sent)
 
 
 def on_device(n, seqs, codes, exponents, w_query, w_key, w_value, norm_gain, w_out):
@@ -265,20 +274,20 @@
     rows = toks // n
     ow = model // OUT_CHUNKS
     steps = seqs.bit_length() - 1
-    x = (codes.astype(F32) * jnp.exp2(exponents.astype(F32))[:, None]).astype(BF)
     hbm = pl.BlockSpec(memory_space=pl.ANY)
     vmem = pl.BlockSpec(memory_space=pltpu.VMEM)
     dma = pltpu.SemaphoreType.DMA
     return pl.pallas_call(
         functools.partial(kernel, n, seqs),
         out_shape=jax.ShapeDtypeStruct((rows, model), BF),
-        in_specs=[hbm, hbm, hbm, hbm, vmem, hbm],
+        in_specs=[hbm, vmem, hbm, hbm, hbm, vmem, hbm],
         out_specs=vmem,
         scratch_shapes=[
             pltpu.VMEM((n, toks, feats), BF),
             pltpu.VMEM((3, depth, width), BF),
             pltpu.VMEM((width, model), BF),
             pltpu.VMEM((3, toks, width), F32),
+            pltpu.VMEM((toks, HD), F32),
             pltpu.VMEM((width, HD), F32),
             pltpu.VMEM((width, HD), F32),
             pltpu.VMEM((steps, width, HD), BF),
@@ -303,7 +312,7 @@
             bytes_accessed=2 * (3 * depth * width + width * model),
             transcendentals=2 * toks * width,
         ),
-    )(x, w_query, w_key, w_value, norm_gain.reshape(1, width), w_out)
+    )(codes, exponents.reshape(1, toks), w_query, w_key, w_value, norm_gain.reshape(1, width), w_out)
 
 
 def solution(mesh):

time: 197 us -> 194 us (0.985)
  other arithmetic: 3.12 us -> 0 us
    convert_element_type x1 -> x0, other arithmetic: 2.44 us -> none  [on_device(): (codes.astype(F32) * jnp.exp2(exponents.astype(F32))[:, None]).astype(BF)]
where the time goes in v2:
time: 194 us
  Pallas kernels  191 us (98%)
  local copies, waits for them, and re-layouts  2.29 us (1%)
    pallas_call x1, Pallas kernels, on_device(): pl.pallas_call(functools.partial(kernel, n, seqs), out_shape=jax.ShapeDty...  191 us

profile of v2, /device:TPU:0, one launch (start us, length us, event | category | flops | bytes accessed | tf_op | source)
XLA Modules:
  0.0 193.8 jit_solution(3677611816948242027)
XLA Ops:
  0.0 191.5 %shard_map.73 = bf16[128,4096]{1,0:T(8,128)(2,1)} custom-call(bf16[512,1024]{1,0:T(8,128)(2,1)} %x_ref.1, s32[1,512]{1,0:T(1,128)} %bitcast.3, bf16[4096,1024]{1,0:T(8,128)(2,1)} %wq_ref.1, bf16[4096,1024]{1,0:T(8,128)(2,1)} %wk_ref.1, bf16[4096,1024]{1,0:T(8,128)(2,1)} %wv_ref.1, f32[1,1024]{1,0:T(1,128)} %bitcast.2, bf16[1024,4096]{1,0:T(8,128)(2,1)} %wo_ref.1), custom_call_target="tpu_custom_call" | custom-call | flops 18253611008 | bytes 33554432 | tf_op jit(solution)/shard_map/pallas_call | solution.py:280
  191.5 2.3 %copy.9 = bf16[128,4096]{1,0:T(8,128)(2,1)} copy(bf16[128,4096]{1,0:T(8,128)(2,1)} %shard_map.73) | data formatting | bytes 2097152

commit v3 on v2

--- a/solution.py
+++ b/solution.py
@@ -11,7 +11,6 @@
 MESH = pl.DeviceIdType.MESH
 GATHER_CHUNKS = 4
 OUT_CHUNKS = 8
-WINDOW = 2
 BF = jnp.bfloat16
 F32 = jnp.float32
 
@@ -21,9 +20,10 @@
 
 
 def kernel(
-    n, seqs, x_ref, exp_ref, wq_ref, wk_ref, wv_ref, gain_ref, wo_ref, out_ref,
+    n, seqs, x_ref, exp_ref, wq_ref, wk_ref, wv_ref, gain_ref, wo_ref, out_ref, far,
     xg, w, wo, acc, scale, tot, pre, sbuf, rbuf, part, land,
     x_sem, w_sem, wo_sem, g_send, g_recv, s_send, s_recv, r_send, r_recv,
+    f_send, f_recv, b_send, b_recv, t_send, t_recv, far_sem,
 ):
     z = lax.axis_index("tp")
     s = lax.axis_index("seq")
@@ -35,6 +35,12 @@
     outs = part.shape[0]
     crows = toks // GATHER_CHUNKS
     steps = seqs.bit_length() - 1
+    half = seqs // 2
+    mine_k, core = s // 2, s % 2
+    slice_rows = width // seqs
+    slice_cols = wo.shape[1] // GATHER_CHUNKS
+    donor = (z == 0) | (z == n - 1)
+    helper = (z == 1) | (z == n - 2)
 
     def partner(i):
         d = 1 << i
@@ -65,6 +71,12 @@
     for i in range(steps):
         pl.semaphore_signal(barrier, inc=1, device_id={"seq": partner(i)}, device_id_type=MESH)
 
+    @pl.loop(0, half)
+    def _(k):
+        @pl.when(k != mine_k)
+        def _():
+            pl.semaphore_signal(barrier, inc=1, device_id={"seq": 2 * k + core}, device_id_type=MESH)
+
     @pl.when(z > 0)
     def _():
         pl.semaphore_signal(barrier, inc=1, device_id={"tp": z - 1}, device_id_type=MESH)
@@ -74,7 +86,7 @@
         pl.semaphore_signal(barrier, inc=1, device_id={"tp": z + 1}, device_id_type=MESH)
 
     near = jnp.where(z > 0, 1, 0) + jnp.where(z < n - 1, 1, 0)
-    pl.semaphore_wait(barrier, near + steps)
+    pl.semaphore_wait(barrier, near + steps + half - 1)
 
     def g_copy(b, c, up):
         chunk = xg.at[b, pl.ds(c * crows, crows)]
@@ -127,9 +139,56 @@
                 project(b, m, first)
         return go
 
+    def slice_of(ref, q, c):
+        at = pl.ds(pl.multiple_of(q * slice_rows, slice_rows), slice_rows)
+        return ref.at[at] if c is None else ref.at[at, pl.ds(c * slice_cols, slice_cols)]
+
+    def hand_in(c):
+        return pltpu.make_async_remote_copy(
+            src_ref=slice_of(wo_ref, s, c), dst_ref=slice_of(far, s, c),
+            send_sem=f_send.at[c], recv_sem=f_recv.at[c],
+            device_id={"tp": jnp.where(z == 0, 1, n - 2)}, device_id_type=MESH,
+        )
+
+    def spread(k, c):
+        return pltpu.make_async_remote_copy(
+            src_ref=slice_of(far, s, c), dst_ref=slice_of(far, s, c),
+            send_sem=b_send.at[k, c], recv_sem=b_recv.at[mine_k, c],
+            device_id={"seq": 2 * k + core}, device_id_type=MESH,
+        )
+
+    def spread_came(k, c):
+        piece = slice_of(far, 2 * k + core, c)
+        pltpu.make_async_copy(piece, piece, b_recv.at[k, c]).wait()
+
+    def to_twin(k):
+        piece = slice_of(far, 2 * k + core, None)
+        return pltpu.make_async_remote_copy(
+            src_ref=piece, dst_ref=piece, send_sem=t_send.at[k], recv_sem=t_recv.at[k],
+            device_id={"seq": partner(0)}, device_id_type=MESH,
+        )
+
+    def others(fn):
+        @pl.loop(0, half)
+        def _(k):
+            pl.when(k != mine_k)(lambda: fn(k))
+
+    def spread_slice(c):
+        hand_in(c).wait_recv()
+        others(lambda k: spread(k, c).start())
+
     project_all(True)(z)
     for t in range(1, n):
+        if t == 2:
+            @pl.when(donor)
+            def _():
+                for c in range(GATHER_CHUNKS):
+                    hand_in(c).start()
+
         for c in range(GATHER_CHUNKS):
+            if t == 2:
+                pl.when(helper & (c > 0))(lambda: spread_slice(c - 1))
+
             @pl.when(z - t >= 0)
             def _():
                 g_copy(z - t, c, True).wait_recv()
@@ -139,6 +198,8 @@
             def _():
                 g_copy(z + t, c, False).wait_recv()
                 pass_on(z + t, c, False)
+        if t == 2:
+            pl.when(helper)(lambda: spread_slice(GATHER_CHUNKS - 1))
         each_block(t, project_all(False))
 
     for t in range(n):
@@ -205,8 +266,18 @@
 
     wo_copy.wait()
 
-    def r_copy(c, j, up):
+    def far_copy(b):
+        return pltpu.make_async_copy(
+            far.at[:, pl.ds(b * width, width)], w.at[0, pl.ds(b * width, width)], far_sem.at[b]
+        )
+
+    blocks = wo.shape[1] // width
+    pieces = width // ow
+
+    def r_copy(c, j, up, pre_norm=None):
         src = part.at[c, pl.ds(j * rows, rows)]
+        if pre_norm is not None:
+            src = pre_norm.at[pl.ds(j * rows, rows), pl.ds(c * ow, ow)]
         slot = j if up else jnp.where(z - 1 == j, n, j)
         return pltpu.make_async_remote_copy(
             src_ref=src, dst_ref=land.at[slot, c],
@@ -214,37 +285,96 @@
             device_id={"tp": z + 1 if up else z - 1}, device_id_type=MESH,
         )
 
-    def arrived(c, slot):
+    for k in range(n - 1):
+        for p in range(pieces):
+            pl.when(z == 0)(lambda: r_copy(p, n - 1 - k, True, o).start())
+            pl.when(z == n - 1)(lambda: r_copy(p, k, False, o).start())
+
+    @pl.when(helper)
+    def _():
+        @pl.loop(0, half)
+        def _(k):
+            @pl.when(k != mine_k)
+            def _():
+                for c in range(GATHER_CHUNKS):
+                    spread_came(k, c)
+            to_twin(k).start()
+
+        @pl.loop(0, half)
+        def _(k):
+            piece = slice_of(far, 2 * k + 1 - core, None)
+            pltpu.make_async_copy(piece, piece, t_recv.at[k]).wait()
+
+        for b in range(blocks):
+            far_copy(b).start()
+        for b in range(blocks):
+            far_copy(b).wait()
+
+    def landed(c, slot):
         ref = land.at[slot, c]
         pltpu.make_async_copy(ref, ref, r_recv.at[slot, c]).wait()
+
+    def arrived(c, slot):
+        landed(c, slot)
         return land[slot, c].astype(F32)
 
     def add_landed(c, j):
         mine = pl.ds(j * rows, rows)
         part[c, mine, :] = (part[c, mine, :].astype(F32) + arrived(c, j)).astype(BF)
 
-    def sent(c):
-        for j in range(n):
-            pl.when(z < j)(lambda: r_copy(c, j, True).wait_send())
-            pl.when(z > j)(lambda: r_copy(c, j, False).wait_send())
+    def outer_term(c, slot):
+        total = jnp.zeros((rows, ow), F32)
+        for p in range(pieces):
+            at = pl.ds(pl.multiple_of((c // pieces) * width + p * ow, ow), ow)
+            cols = pl.ds(pl.multiple_of((c % pieces) * ow, ow), ow)
+            total += jnp.dot(land[slot, p], w[0, at, cols], preferred_element_type=F32)
+        return total
+
+    def add_outer(c, j):
+        mine = pl.ds(j * rows, rows)
+        part[c, mine, :] = (part[c, mine, :].astype(F32) + outer_term(c, j)).astype(BF)
 
     @pl.loop(0, outs)
     def _(c):
         cols = pl.ds(pl.multiple_of(c * ow, ow), ow)
         part[c] = jnp.dot(o[...], wo[:, cols], preferred_element_type=F32).astype(BF)
-        pl.when(c >= WINDOW)(lambda: sent(c - WINDOW))
-        for k in range(n - 1):
-            up_j, down_j = n - 1 - k, k
-
-            @pl.when(z < up_j)
-            def _():
-                pl.when(z > 0)(lambda: add_landed(c, up_j))
+
+    for k in range(n - 2):
+        up_j, down_j = n - 1 - k, k
+
+        @pl.when(z == 1)
+        def _():
+            for p in range(pieces):
+                landed(p, up_j)
+
+        @pl.when(z == n - 2)
+        def _():
+            for p in range(pieces):
+                landed(p, down_j)
+
+        @pl.loop(0, outs)
+        def _(c):
+            @pl.when((z < up_j) & (z > 0))
+            def _():
+                pl.when(z > 1)(lambda: add_landed(c, up_j))
+                pl.when(z == 1)(lambda: add_outer(c, up_j))
                 r_copy(c, up_j, True).start()
 
-            @pl.when(z > down_j)
-            def _():
-                pl.when(z < n - 1)(lambda: add_landed(c, down_j))
+            @pl.when((z > down_j) & (z < n - 1))
+            def _():
+                pl.when(z < n - 2)(lambda: add_landed(c, down_j))
+                pl.when(z == n - 2)(lambda: add_outer(c, down_j))
                 r_copy(c, down_j, False).start()
+
+    @pl.when(z == 1)
+    def _():
+        for p in range(pieces):
+            landed(p, 1)
+
+    @pl.when(z == n - 2)
+    def _():
+        for p in range(pieces):
+            landed(p, n)
 
     @pl.loop(0, outs)
     def _(c):
@@ -260,11 +390,44 @@
         def _():
             out_ref[:, cols] = (total + arrived(c, n - 1)).astype(BF)
 
-        @pl.when((z > 0) & (z < n - 1))
-        def _():
-            out_ref[:, cols] = (total + arrived(c, z) + arrived(c, n)).astype(BF)
-
-    pl.loop(outs - WINDOW, outs)(sent)
+        @pl.when(z == 1)
+        def _():
+            out_ref[:, cols] = (total + outer_term(c, 1) + arrived(c, n)).astype(BF)
+
+        @pl.when(z == n - 2)
+        def _():
+            out_ref[:, cols] = (total + outer_term(c, n) + arrived(c, n - 2)).astype(BF)
+
+        if n > 4:
+            @pl.when((z > 1) & (z < n - 2))
+            def _():
+                out_ref[:, cols] = (total + arrived(c, z) + arrived(c, n)).astype(BF)
+
+    @pl.loop(0, outs)
+    def _(c):
+        for j in range(n):
+            pl.when((z < j) & (z > 0))(lambda: r_copy(c, j, True).wait_send())
+            pl.when((z > j) & (z < n - 1))(lambda: r_copy(c, j, False).wait_send())
+
+    for k in range(n - 1):
+        for p in range(pieces):
+            pl.when(z == 0)(lambda: r_copy(p, n - 1 - k, True, o).wait_send())
+            pl.when(z == n - 1)(lambda: r_copy(p, k, False, o).wait_send())
+
+    @pl.when(donor)
+    def _():
+        for c in range(GATHER_CHUNKS):
+            hand_in(c).wait_send()
+
+    @pl.when(helper)
+    def _():
+        @pl.loop(0, half)
+        def _(k):
+            @pl.when(k != mine_k)
+            def _():
+                for c in range(GATHER_CHUNKS):
+                    spread(k, c).wait_send()
+            to_twin(k).wait_send()
 
 
 def on_device(n, seqs, codes, exponents, w_query, w_key, w_value, norm_gain, w_out):
@@ -279,9 +442,9 @@
     dma = pltpu.SemaphoreType.DMA
     return pl.pallas_call(
         functools.partial(kernel, n, seqs),
-        out_shape=jax.ShapeDtypeStruct((rows, model), BF),
+        out_shape=(jax.ShapeDtypeStruct((rows, model), BF), jax.ShapeDtypeStruct((width, model), BF)),
         in_specs=[hbm, vmem, hbm, hbm, hbm, vmem, hbm],
-        out_specs=vmem,
+        out_specs=(vmem, hbm),
         scratch_shapes=[
             pltpu.VMEM((n, toks, feats), BF),
             pltpu.VMEM((3, depth, width), BF),
@@ -303,6 +466,13 @@
             dma((steps,)),
             dma((n, OUT_CHUNKS)),
             dma((n + 1, OUT_CHUNKS)),
+            dma((GATHER_CHUNKS,)),
+            dma((GATHER_CHUNKS,)),
+            dma((seqs // 2, GATHER_CHUNKS)),
+            dma((seqs // 2, GATHER_CHUNKS)),
+            dma((seqs // 2,)),
+            dma((seqs // 2,)),
+            dma((model // width,)),
         ],
         compiler_params=pltpu.CompilerParams(
             collective_id=0, has_side_effects=True, vmem_limit_bytes=62 * 1024 * 1024
@@ -312,7 +482,7 @@
             bytes_accessed=2 * (3 * depth * width + width * model),
             transcendentals=2 * toks * width,
         ),
-    )(codes, exponents.reshape(1, toks), w_query, w_key, w_value, norm_gain.reshape(1, width), w_out)
+    )(codes, exponents.reshape(1, toks), w_query, w_key, w_value, norm_gain.reshape(1, width), w_out)[0]
 
 
 def solution(mesh):

time: 194 us -> 206 us (1.062)
  the two profiles are of different devices: /device:TPU:0 before, /device:TPU:12 now
where the time goes in v3:
time: 206 us; the launch traced here: 204 us
  Pallas kernels  202 us (98%)
  local copies, waits for them, and re-layouts  2.29 us (1%)
    pallas_call x1, Pallas kernels, on_device(): pl.pallas_call(functools.partial(kernel, n, seqs), out_shape=(jax.ShapeDt...  202 us

profile of v3, /device:TPU:12, one launch (start us, length us, event | category | flops | bytes accessed | tf_op | source)
XLA Modules:
  0.0 204.1 jit_solution(10385191943372538423)
XLA Ops:
  0.0 201.8 %shard_map.73 = (bf16[128,4096]{1,0:T(8,128)(2,1)}, bf16[1024,4096]{1,0:T(8,128)(2,1)}) custom-call(bf16[512,1024]{1,0:T(8,128)(2,1)} %x_ref.1, s32[1,512]{1,0:T(1,128)} %bitcast.3, bf16[4096,1024]{1,0:T(8,128)(2,1)} %wq_ref.1, bf16[4096,1024]{1,0:T(8,128)(2,1)} %wk_ref.1, bf16[4096,1024]{1,0:T(8,128)(2,1)} %wv_ref.1, f32[1,1024]{1,0:T(1,128)} %bitcast.2, ...), custom_call_target="tpu_custom_call" | custom-call | flops 18253611008 | bytes 33554432 | tf_op jit(solution)/shard_map/pallas_call | solution.py:443
  201.8 2.3 %copy.9 = bf16[128,4096]{1,0:T(8,128)(2,1)} copy(bf16[128,4096]{1,0:T(8,128)(2,1)} %get-tuple-element.6) | data formatting | bytes 2097152

commit v4 on v3

--- a/solution.py
+++ b/solution.py
@@ -54,12 +54,20 @@
         block = pl.ds(pl.multiple_of(b * feats, feats), feats)
         return pltpu.make_async_copy(src.at[block], w.at[m, block], w_sem.at[m, b])
 
+    def from_below(t):
+        late = (z == 1) if t == 2 else (z < 0)
+        return ((z >= t) & (z != 1)) | late, jnp.where(z == 1, 0, z - t)
+
+    def from_above(t):
+        late = (z == n - 2) if t == 2 else (z < 0)
+        return ((z + t < n) & (z != n - 2)) | late, jnp.where(z == n - 2, n - 1, z + t)
+
     def each_block(t, fn):
         if t == 0:
             fn(z)
             return
-        pl.when(z - t >= 0)(lambda: fn(z - t))
-        pl.when(z + t < n)(lambda: fn(z + t))
+        pl.when(from_below(t)[0])(lambda: fn(from_below(t)[1]))
+        pl.when(from_above(t)[0])(lambda: fn(from_above(t)[1]))
 
     def start_w(b):
         for m in range(3):
@@ -102,10 +110,63 @@
         else:
             pl.when(z > 0)(lambda: g_copy(b, c, False).start())
 
-    own.wait()
-    for c in range(GATHER_CHUNKS):
+    def slice_of(ref, q, c):
+        at = pl.ds(pl.multiple_of(q * slice_rows, slice_rows), slice_rows)
+        return ref.at[at] if c is None else ref.at[at, pl.ds(c * slice_cols, slice_cols)]
+
+    def hand_in(c):
+        return pltpu.make_async_remote_copy(
+            src_ref=slice_of(wo_ref, s, c), dst_ref=slice_of(far, s, c),
+            send_sem=f_send.at[c], recv_sem=f_recv.at[c],
+            device_id={"tp": jnp.where(z == 0, 1, n - 2)}, device_id_type=MESH,
+        )
+
+    def spread(k, c):
+        return pltpu.make_async_remote_copy(
+            src_ref=slice_of(far, s, c), dst_ref=slice_of(far, s, c),
+            send_sem=b_send.at[k, c], recv_sem=b_recv.at[mine_k, c],
+            device_id={"seq": 2 * k + core}, device_id_type=MESH,
+        )
+
+    def spread_came(k, c):
+        piece = slice_of(far, 2 * k + core, c)
+        pltpu.make_async_copy(piece, piece, b_recv.at[k, c]).wait()
+
+    def to_twin(k):
+        piece = slice_of(far, 2 * k + core, None)
+        return pltpu.make_async_remote_copy(
+            src_ref=piece, dst_ref=piece, send_sem=t_send.at[k], recv_sem=t_recv.at[k],
+            device_id={"seq": partner(0)}, device_id_type=MESH,
+        )
+
+    def others(fn):
+        @pl.loop(0, half)
+        def _(k):
+            pl.when(k != mine_k)(lambda: fn(k))
+
+    def spread_slice(c):
+        hand_in(c).wait_recv()
+        others(lambda k: spread(k, c).start())
+
+    def send_own(c):
         pass_on(z, c, True)
         pass_on(z, c, False)
+
+    def own_sent(c):
+        pl.when(z == 0)(lambda: g_copy(z, c, True).wait_send())
+        pl.when(z == n - 1)(lambda: g_copy(z, c, False).wait_send())
+
+    own.wait()
+
+    @pl.when(donor)
+    def _():
+        for c in range(GATHER_CHUNKS):
+            hand_in(c).start()
+
+    @pl.when((z > 0) & (z < n - 1))
+    def _():
+        for c in range(GATHER_CHUNKS):
+            send_own(c)
 
     for t in range(1, n):
         each_block(t, start_w)
@@ -139,78 +200,49 @@
                 project(b, m, first)
         return go
 
-    def slice_of(ref, q, c):
-        at = pl.ds(pl.multiple_of(q * slice_rows, slice_rows), slice_rows)
-        return ref.at[at] if c is None else ref.at[at, pl.ds(c * slice_cols, slice_cols)]
-
-    def hand_in(c):
-        return pltpu.make_async_remote_copy(
-            src_ref=slice_of(wo_ref, s, c), dst_ref=slice_of(far, s, c),
-            send_sem=f_send.at[c], recv_sem=f_recv.at[c],
-            device_id={"tp": jnp.where(z == 0, 1, n - 2)}, device_id_type=MESH,
-        )
-
-    def spread(k, c):
-        return pltpu.make_async_remote_copy(
-            src_ref=slice_of(far, s, c), dst_ref=slice_of(far, s, c),
-            send_sem=b_send.at[k, c], recv_sem=b_recv.at[mine_k, c],
-            device_id={"seq": 2 * k + core}, device_id_type=MESH,
-        )
-
-    def spread_came(k, c):
-        piece = slice_of(far, 2 * k + core, c)
-        pltpu.make_async_copy(piece, piece, b_recv.at[k, c]).wait()
-
-    def to_twin(k):
-        piece = slice_of(far, 2 * k + core, None)
-        return pltpu.make_async_remote_copy(
-            src_ref=piece, dst_ref=piece, send_sem=t_send.at[k], recv_sem=t_recv.at[k],
-            device_id={"seq": partner(0)}, device_id_type=MESH,
-        )
-
-    def others(fn):
-        @pl.loop(0, half)
-        def _(k):
-            pl.when(k != mine_k)(lambda: fn(k))
-
-    def spread_slice(c):
-        hand_in(c).wait_recv()
-        others(lambda k: spread(k, c).start())
-
     project_all(True)(z)
     for t in range(1, n):
         if t == 2:
             @pl.when(donor)
             def _():
                 for c in range(GATHER_CHUNKS):
-                    hand_in(c).start()
-
+                    own_sent(c)
+                    if c + 2 < GATHER_CHUNKS:
+                        send_own(c + 2)
+
+        below, low = from_below(t)
+        above, high = from_above(t)
         for c in range(GATHER_CHUNKS):
-            if t == 2:
-                pl.when(helper & (c > 0))(lambda: spread_slice(c - 1))
-
-            @pl.when(z - t >= 0)
-            def _():
-                g_copy(z - t, c, True).wait_recv()
-                pass_on(z - t, c, True)
-
-            @pl.when(z + t < n)
-            def _():
-                g_copy(z + t, c, False).wait_recv()
-                pass_on(z + t, c, False)
-        if t == 2:
-            pl.when(helper)(lambda: spread_slice(GATHER_CHUNKS - 1))
+            @pl.when(below)
+            def _():
+                g_copy(low, c, True).wait_recv()
+                pass_on(low, c, True)
+
+            @pl.when(above)
+            def _():
+                g_copy(high, c, False).wait_recv()
+                pass_on(high, c, False)
+
+            if t == 1:
+                pl.when(helper)(lambda: spread_slice(c))
+        if t == 1:
+            @pl.when(donor)
+            def _():
+                for c in range(GATHER_CHUNKS):
+                    hand_in(c).wait_send()
+                for c in range(2):
+                    send_own(c)
         each_block(t, project_all(False))
 
-    for t in range(n):
-        for c in range(GATHER_CHUNKS):
-            @pl.when((z - t >= 0) & (z < n - 1))
-            def _():
-                g_copy(z - t, c, True).wait_send()
-
-            @pl.when((z + t < n) & (z > 0))
-            def _():
-                g_copy(z + t, c, False).wait_send()
+    for c in range(GATHER_CHUNKS):
+        @pl.when((z > 0) & (z < n - 1))
+        def _():
+            g_copy(z, c, True).wait_send()
+            g_copy(z, c, False).wait_send()
+
+        for t in range(1, n):
+            pl.when(from_below(t)[0] & (z < n - 1))(lambda: g_copy(from_below(t)[1], c, True).wait_send())
+            pl.when(from_above(t)[0] & (z > 0))(lambda: g_copy(from_above(t)[1], c, False).wait_send())
 
     fk, vb, fq, o = xg.at[0], xg.at[1], xg.at[2], xg.at[3]
 
@@ -413,11 +445,6 @@
         for p in range(pieces):
             pl.when(z == 0)(lambda: r_copy(p, n - 1 - k, True, o).wait_send())
             pl.when(z == n - 1)(lambda: r_copy(p, k, False, o).wait_send())
-
-    @pl.when(donor)
-    def _():
-        for c in range(GATHER_CHUNKS):
-            hand_in(c).wait_send()
 
     @pl.when(helper)
     def _():

time: 206 us -> 225 us (1.092)
  Pallas kernels: 202 us -> 220 us
    pallas_call x1, Pallas kernels: 202 us -> 220 us  [on_device(): pl.pallas_call(functools.partial(kernel, n, seqs), out_shape=(jax.ShapeDt...]
where the time goes in v4:
time: 225 us; the launch traced here: 223 us
  Pallas kernels  220 us (98%)
  local copies, waits for them, and re-layouts  2.29 us (1%)
    pallas_call x1, Pallas kernels, on_device(): pl.pallas_call(functools.partial(kernel, n, seqs), out_shape=(jax.ShapeDt...  220 us

profile of v4, /device:TPU:12, one launch (start us, length us, event | category | flops | bytes accessed | tf_op | source)
XLA Modules:
  0.0 222.7 jit_solution(776658088848975774)
XLA Ops:
  0.0 220.4 %shard_map.73 = (bf16[128,4096]{1,0:T(8,128)(2,1)}, bf16[1024,4096]{1,0:T(8,128)(2,1)}) custom-call(bf16[512,1024]{1,0:T(8,128)(2,1)} %x_ref.1, s32[1,512]{1,0:T(1,128)} %bitcast.3, bf16[4096,1024]{1,0:T(8,128)(2,1)} %wq_ref.1, bf16[4096,1024]{1,0:T(8,128)(2,1)} %wk_ref.1, bf16[4096,1024]{1,0:T(8,128)(2,1)} %wv_ref.1, f32[1,1024]{1,0:T(1,128)} %bitcast.2, ...), custom_call_target="tpu_custom_call" | custom-call | flops 18253611008 | bytes 33554432 | tf_op jit(solution)/shard_map/pallas_call | solution.py:470
  220.4 2.3 %copy.9 = bf16[128,4096]{1,0:T(8,128)(2,1)} copy(bf16[128,4096]{1,0:T(8,128)(2,1)} %get-tuple-element.6) | data formatting | bytes 2097152

commit v5 on v2

--- a/solution.py
+++ b/solution.py
@@ -12,6 +12,7 @@
 GATHER_CHUNKS = 4
 OUT_CHUNKS = 8
 WINDOW = 2
+LAG = 3
 BF = jnp.bfloat16
 F32 = jnp.float32
 
@@ -23,7 +24,7 @@
 def kernel(
     n, seqs, x_ref, exp_ref, wq_ref, wk_ref, wv_ref, gain_ref, wo_ref, out_ref,
     xg, w, wo, acc, scale, tot, pre, sbuf, rbuf, part, land,
-    x_sem, w_sem, wo_sem, g_send, g_recv, s_send, s_recv, r_send, r_recv,
+    got, exps, gate, x_sem, swap_send, swap_recv, e_send, e_recv, back_send, back_recv, w_sem, wo_sem, g_send, g_recv, s_send, s_recv, r_send, r_recv,
 ):
     z = lax.axis_index("tp")
     s = lax.axis_index("seq")
@@ -34,14 +35,28 @@
     ow = part.shape[2]
     outs = part.shape[0]
     crows = toks // GATHER_CHUNKS
-    steps = seqs.bit_length() - 1
+    half = seqs // 2
+    steps = half.bit_length() - 1
+    late = s % 2 == 1
+    early = s % 2 == 0
+    twin = s + 1 - 2 * (s % 2)
+    trades = jnp.where(s < half, s % 2, 1 - s % 2) == 1
+    keeps = jnp.where(s < half, s % 2, 1 - s % 2) == 0
+    mate = jnp.where(s < half, s + half - 1, s - half + 1)
+    shard = jnp.where(trades, mate, s)
+
+    def holder(u):
+        first = jnp.where(u % 2 == 0, u, u + half - 1)
+        second = jnp.where(u % 2 == 1, u, u - half + 1)
+        return jnp.where(u < half, first, second)
 
     def partner(i):
         d = 1 << i
-        return s + d * (1 - 2 * ((s // d) % 2))
+        return holder(shard + d * (1 - 2 * ((shard // d) % 2)))
 
     own = pltpu.make_async_copy(x_ref, xg.at[z], x_sem)
-    own.start()
+    pl.when(keeps)(lambda: own.start())
+    exps[0] = jnp.broadcast_to(exp_ref[...].astype(F32), exps.shape[1:])
 
     def w_copy(m, b):
         src = (wq_ref, wk_ref, wv_ref)[m]
@@ -65,6 +80,12 @@
     for i in range(steps):
         pl.semaphore_signal(barrier, inc=1, device_id={"seq": partner(i)}, device_id_type=MESH)
 
+    pl.semaphore_signal(barrier, inc=1, device_id={"seq": twin}, device_id_type=MESH)
+
+    @pl.when(trades)
+    def _():
+        pl.semaphore_signal(barrier, inc=1, device_id={"seq": mate}, device_id_type=MESH)
+
     @pl.when(z > 0)
     def _():
         pl.semaphore_signal(barrier, inc=1, device_id={"tp": z - 1}, device_id_type=MESH)
@@ -74,7 +95,25 @@
         pl.semaphore_signal(barrier, inc=1, device_id={"tp": z + 1}, device_id_type=MESH)
 
     near = jnp.where(z > 0, 1, 0) + jnp.where(z < n - 1, 1, 0)
-    pl.semaphore_wait(barrier, near + steps)
+    pl.semaphore_wait(barrier, near + steps + 1 + jnp.where(trades, 1, 0))
+
+    def swap(c):
+        at = pl.ds(c * crows, crows)
+        return pltpu.make_async_remote_copy(
+            src_ref=x_ref.at[at], dst_ref=xg.at[z, at], send_sem=swap_send.at[c], recv_sem=swap_recv.at[c],
+            device_id={"seq": mate}, device_id_type=MESH,
+        )
+
+    e_copy = pltpu.make_async_remote_copy(
+        src_ref=exps.at[0], dst_ref=exps.at[1], send_sem=e_send, recv_sem=e_recv,
+        device_id={"seq": mate}, device_id_type=MESH,
+    )
+
+    @pl.when(trades)
+    def _():
+        for c in range(GATHER_CHUNKS):
+            swap(c).start()
+        e_copy.start()
 
     def g_copy(b, c, up):
         chunk = xg.at[b, pl.ds(c * crows, crows)]
@@ -90,10 +129,21 @@
         else:
             pl.when(z > 0)(lambda: g_copy(b, c, False).start())
 
-    own.wait()
-    for c in range(GATHER_CHUNKS):
+    def send_own(c):
         pass_on(z, c, True)
         pass_on(z, c, False)
+
+    pl.when(keeps)(lambda: own.wait())
+    for c in range(GATHER_CHUNKS):
+        pl.when(trades)(lambda: swap(c).wait_recv())
+        pl.when(early)(lambda: send_own(c))
+
+    @pl.when(trades)
+    def _():
+        e_copy.wait()
+        exps[0] = exps[1]
+        for c in range(GATHER_CHUNKS):
+            swap(c).wait_send()
 
     for t in range(1, n):
         each_block(t, start_w)
@@ -103,7 +153,7 @@
     on_diagonal = lax.broadcasted_iota(jnp.int32, (toks, toks), 0) == lax.broadcasted_iota(
         jnp.int32, (toks, toks), 1
     )
-    row_scale = jnp.where(on_diagonal, jnp.exp2(exp_ref[...].astype(F32)), 0.0)
+    row_scale = jnp.where(on_diagonal, jnp.exp2(exps[0, 0:1, :]), 0.0)
     scale[...] = jnp.broadcast_to(jnp.sum(row_scale, axis=1, keepdims=True), scale.shape)
 
     tile = min(256, width)
@@ -128,6 +178,13 @@
         return go
 
     project_all(True)(z)
+
+    @pl.when(late)
+    def _():
+        pl.semaphore_wait(gate, 1)
+        for c in range(GATHER_CHUNKS):
+            send_own(c)
+
     for t in range(1, n):
         for c in range(GATHER_CHUNKS):
             @pl.when(z - t >= 0)
@@ -150,6 +207,10 @@
             @pl.when((z + t < n) & (z > 0))
             def _():
                 g_copy(z + t, c, False).wait_send()
+
+    @pl.when(early)
+    def _():
+        pl.semaphore_signal(gate, inc=1, device_id={"seq": twin}, device_id_type=MESH)
 
     fk, vb, fq, o = xg.at[0], xg.at[1], xg.at[2], xg.at[3]
 
@@ -192,9 +253,24 @@
         came = rbuf[i].astype(F32)
         tot[...] += came
 
-        @pl.when((s // (1 << i)) % 2 == 1)
+        @pl.when((shard // (1 << i)) % 2 == 1)
         def _():
             pre[...] += came
+
+    first_half = pltpu.make_async_remote_copy(
+        src_ref=sbuf.at[steps], dst_ref=rbuf.at[steps], send_sem=s_send.at[steps], recv_sem=s_recv.at[steps],
+        device_id={"seq": twin}, device_id_type=MESH,
+    )
+
+    @pl.when(early)
+    def _():
+        sbuf[steps] = tot[...].astype(BF)
+        first_half.start()
+
+    @pl.when(late)
+    def _():
+        first_half.wait_recv()
+        pre[...] += rbuf[steps].astype(F32)
 
     @pl.loop(0, heads)
     def _(h):
@@ -214,14 +290,47 @@
             device_id={"tp": z + 1 if up else z - 1}, device_id_type=MESH,
         )
 
-    def arrived(c, slot):
+    def landed(c, slot):
         ref = land.at[slot, c]
         pltpu.make_async_copy(ref, ref, r_recv.at[slot, c]).wait()
+
+    def arrived(c, slot):
+        landed(c, slot)
         return land[slot, c].astype(F32)
 
     def add_landed(c, j):
         mine = pl.ds(j * rows, rows)
         part[c, mine, :] = (part[c, mine, :].astype(F32) + arrived(c, j)).astype(BF)
+
+    def back(c):
+        mine = pl.ds(pl.multiple_of(z * rows, rows), rows)
+        return pltpu.make_async_remote_copy(
+            src_ref=part.at[c, mine], dst_ref=got.at[c], send_sem=back_send.at[c], recv_sem=back_recv.at[c],
+            device_id={"seq": mate}, device_id_type=MESH,
+        )
+
+    def finish(c):
+        cols = pl.ds(pl.multiple_of(c * ow, ow), ow)
+        mine = pl.ds(pl.multiple_of(z * rows, rows), rows)
+        pl.when(z > 0)(lambda: landed(c, z))
+        pl.when(z < n - 1)(lambda: landed(c, n))
+
+        def give(total):
+            @pl.when(keeps)
+            def _():
+                out_ref[:, cols] = total.astype(BF)
+
+            @pl.when(trades)
+            def _():
+                part[c, mine, :] = total.astype(BF)
+
+        total = part[c, mine, :].astype(F32)
+        pl.when(z == 0)(lambda: give(total + land[n, c].astype(F32)))
+        pl.when(z == n - 1)(lambda: give(total + land[n - 1, c].astype(F32)))
+        pl.when((z > 0) & (z < n - 1))(
+            lambda: give(total + land[z, c].astype(F32) + land[n, c].astype(F32))
+        )
+        pl.when(trades)(lambda: back(c).start())
 
     def sent(c):
         for j in range(n):
@@ -245,26 +354,19 @@
             def _():
                 pl.when(z < n - 1)(lambda: add_landed(c, down_j))
                 r_copy(c, down_j, False).start()
-
-    @pl.loop(0, outs)
-    def _(c):
-        cols = pl.ds(pl.multiple_of(c * ow, ow), ow)
-        mine = pl.ds(pl.multiple_of(z * rows, rows), rows)
-        total = part[c, mine, :].astype(F32)
-
-        @pl.when(z == 0)
-        def _():
-            out_ref[:, cols] = (total + arrived(c, n)).astype(BF)
-
-        @pl.when(z == n - 1)
-        def _():
-            out_ref[:, cols] = (total + arrived(c, n - 1)).astype(BF)
-
-        @pl.when((z > 0) & (z < n - 1))
-        def _():
-            out_ref[:, cols] = (total + arrived(c, z) + arrived(c, n)).astype(BF)
-
+        pl.when(c >= LAG)(lambda: finish(c - LAG))
+
+    pl.loop(outs - LAG, outs)(finish)
     pl.loop(outs - WINDOW, outs)(sent)
+
+    @pl.when(trades)
+    def _():
+        @pl.loop(0, outs)
+        def _(c):
+            back(c).wait()
+            out_ref[:, pl.ds(pl.multiple_of(c * ow, ow), ow)] = got[c]
+
+    pl.when(early)(lambda: first_half.wait_send())
 
 
 def on_device(n, seqs, codes, exponents, w_query, w_key, w_value, norm_gain, w_out):
@@ -273,7 +375,7 @@
     model = w_out.shape[1]
     rows = toks // n
     ow = model // OUT_CHUNKS
-    steps = seqs.bit_length() - 1
+    steps = (seqs // 2).bit_length() - 1
     hbm = pl.BlockSpec(memory_space=pl.ANY)
     vmem = pl.BlockSpec(memory_space=pltpu.VMEM)
     dma = pltpu.SemaphoreType.DMA
@@ -290,17 +392,26 @@
             pltpu.VMEM((toks, HD), F32),
             pltpu.VMEM((width, HD), F32),
             pltpu.VMEM((width, HD), F32),
-            pltpu.VMEM((steps, width, HD), BF),
-            pltpu.VMEM((steps, width, HD), BF),
+            pltpu.VMEM((steps + 1, width, HD), BF),
+            pltpu.VMEM((steps + 1, width, HD), BF),
             pltpu.VMEM((OUT_CHUNKS, toks, ow), BF),
             pltpu.VMEM((n + 1, OUT_CHUNKS, rows, ow), BF),
+            pltpu.VMEM((OUT_CHUNKS, rows, ow), BF),
+            pltpu.VMEM((2, 8, toks), F32),
+            pltpu.SemaphoreType.REGULAR,
             dma(()),
+            dma((GATHER_CHUNKS,)),
+            dma((GATHER_CHUNKS,)),
+            dma(()),
+            dma(()),
+            dma((OUT_CHUNKS,)),
+            dma((OUT_CHUNKS,)),
             dma((3, n)),
             dma(()),
             dma((2, n, GATHER_CHUNKS)),
             dma((n, GATHER_CHUNKS)),
-            dma((steps,)),
-            dma((steps,)),
+            dma((steps + 1,)),
+            dma((steps + 1,)),
             dma((n, OUT_CHUNKS)),
             dma((n + 1, OUT_CHUNKS)),
         ],

time: 194 us -> 195 us (level)
  the two profiles are of different devices: /device:TPU:0 before, /device:TPU:12 now
where the time goes in v5:
time: 195 us
  Pallas kernels  192 us (98%)
  local copies, waits for them, and re-layouts  2.29 us (1%)
    pallas_call x1, Pallas kernels, on_device(): pl.pallas_call(functools.partial(kernel, n, seqs), out_shape=jax.ShapeDty...  192 us

profile of v5, /device:TPU:12, one launch (start us, length us, event | category | flops | bytes accessed | tf_op | source)
XLA Modules:
  0.0 194.5 jit_solution(1734403388981624662)
XLA Ops:
  0.0 192.2 %shard_map.73 = bf16[128,4096]{1,0:T(8,128)(2,1)} custom-call(bf16[512,1024]{1,0:T(8,128)(2,1)} %x_ref.1, s32[1,512]{1,0:T(1,128)} %bitcast.3, bf16[4096,1024]{1,0:T(8,128)(2,1)} %wq_ref.1, bf16[4096,1024]{1,0:T(8,128)(2,1)} %wk_ref.1, bf16[4096,1024]{1,0:T(8,128)(2,1)} %wv_ref.1, f32[1,1024]{1,0:T(1,128)} %bitcast.2, bf16[1024,4096]{1,0:T(8,128)(2,1)} %wo_ref.1), custom_call_target="tpu_custom_call" | custom-call | flops 18253611008 | bytes 33554432 | tf_op jit(solution)/shard_map/pallas_call | solution.py:382
  192.2 2.3 %copy.9 = bf16[128,4096]{1,0:T(8,128)(2,1)} copy(bf16[128,4096]{1,0:T(8,128)(2,1)} %shard_map.73) | data formatting | bytes 2097152

commit v6 on v5

--- a/solution.py
+++ b/solution.py
@@ -11,7 +11,7 @@
 MESH = pl.DeviceIdType.MESH
 GATHER_CHUNKS = 4
 OUT_CHUNKS = 8
-WINDOW = 2
+WINDOW = 4
 LAG = 3
 BF = jnp.bfloat16
 F32 = jnp.float32
@@ -156,7 +156,7 @@
     row_scale = jnp.where(on_diagonal, jnp.exp2(exps[0, 0:1, :]), 0.0)
     scale[...] = jnp.broadcast_to(jnp.sum(row_scale, axis=1, keepdims=True), scale.shape)
 
-    tile = min(256, width)
+    tile = min(512, width)
 
     def project(b, m, first):
         w_copy(m, b).wait()
@@ -196,6 +196,11 @@
             def _():
                 g_copy(z + t, c, False).wait_recv()
                 pass_on(z + t, c, False)
+        if t == max(n - 2, 1):
+            @pl.when(early)
+            def _():
+                pl.semaphore_signal(gate, inc=1, device_id={"seq": twin}, device_id_type=MESH)
+
         each_block(t, project_all(False))
 
     for t in range(n):
@@ -207,10 +212,6 @@
             @pl.when((z + t < n) & (z > 0))
             def _():
                 g_copy(z + t, c, False).wait_send()
-
-    @pl.when(early)
-    def _():
-        pl.semaphore_signal(gate, inc=1, device_id={"seq": twin}, device_id_type=MESH)
 
     fk, vb, fq, o = xg.at[0], xg.at[1], xg.at[2], xg.at[3]
 

time: 195 us -> 186 us (0.954)
  Pallas kernels: 192 us -> 184 us
    pallas_call x1, Pallas kernels: 192 us -> 184 us  [on_device(): pl.pallas_call(functools.partial(kernel, n, seqs), out_shape=jax.ShapeDty...]
where the time goes in v6:
time: 186 us
  Pallas kernels  184 us (99%)
  local copies, waits for them, and re-layouts  2.29 us (1%)
    pallas_call x1, Pallas kernels, on_device(): pl.pallas_call(functools.partial(kernel, n, seqs), out_shape=jax.ShapeDty...  184 us

profile of v6, /device:TPU:12, one launch (start us, length us, event | category | flops | bytes accessed | tf_op | source)
XLA Modules:
  0.0 186.0 jit_solution(15389636845669002895)
XLA Ops:
  0.0 183.7 %shard_map.73 = bf16[128,4096]{1,0:T(8,128)(2,1)} custom-call(bf16[512,1024]{1,0:T(8,128)(2,1)} %x_ref.1, s32[1,512]{1,0:T(1,128)} %bitcast.3, bf16[4096,1024]{1,0:T(8,128)(2,1)} %wq_ref.1, bf16[4096,1024]{1,0:T(8,128)(2,1)} %wk_ref.1, bf16[4096,1024]{1,0:T(8,128)(2,1)} %wv_ref.1, f32[1,1024]{1,0:T(1,128)} %bitcast.2, bf16[1024,4096]{1,0:T(8,128)(2,1)} %wo_ref.1), custom_call_target="tpu_custom_call" | custom-call | flops 18253611008 | bytes 33554432 | tf_op jit(solution)/shard_map/pallas_call | solution.py:383
  183.7 2.3 %copy.9 = bf16[128,4096]{1,0:T(8,128)(2,1)} copy(bf16[128,4096]{1,0:T(8,128)(2,1)} %shard_map.73) | data formatting | bytes 2097152

commit v7 on v6

--- a/solution.py
+++ b/solution.py
@@ -196,7 +196,7 @@
             def _():
                 g_copy(z + t, c, False).wait_recv()
                 pass_on(z + t, c, False)
-        if t == max(n - 2, 1):
+        if t == 1:
             @pl.when(early)
             def _():
                 pl.semaphore_signal(gate, inc=1, device_id={"seq": twin}, device_id_type=MESH)

time: 186 us -> 190 us (1.022)
  Pallas kernels: 184 us -> 188 us
    pallas_call x1, Pallas kernels: 184 us -> 188 us  [on_device(): pl.pallas_call(functools.partial(kernel, n, seqs), out_shape=jax.ShapeDty...]
where the time goes in v7:
time: 190 us
  Pallas kernels  188 us (99%)
  local copies, waits for them, and re-layouts  2.29 us (1%)
    pallas_call x1, Pallas kernels, on_device(): pl.pallas_call(functools.partial(kernel, n, seqs), out_shape=jax.ShapeDty...  188 us

profile of v7, /device:TPU:12, one launch (start us, length us, event | category | flops | bytes accessed | tf_op | source)
XLA Modules:
  0.0 190.2 jit_solution(17105944432191846674)
XLA Ops:
  0.0 188.0 %shard_map.73 = bf16[128,4096]{1,0:T(8,128)(2,1)} custom-call(bf16[512,1024]{1,0:T(8,128)(2,1)} %x_ref.1, s32[1,512]{1,0:T(1,128)} %bitcast.3, bf16[4096,1024]{1,0:T(8,128)(2,1)} %wq_ref.1, bf16[4096,1024]{1,0:T(8,128)(2,1)} %wk_ref.1, bf16[4096,1024]{1,0:T(8,128)(2,1)} %wv_ref.1, f32[1,1024]{1,0:T(1,128)} %bitcast.2, bf16[1024,4096]{1,0:T(8,128)(2,1)} %wo_ref.1), custom_call_target="tpu_custom_call" | custom-call | flops 18253611008 | bytes 33554432 | tf_op jit(solution)/shard_map/pallas_call | solution.py:383
  188.0 2.3 %copy.9 = bf16[128,4096]{1,0:T(8,128)(2,1)} copy(bf16[128,4096]{1,0:T(8,128)(2,1)} %shard_map.73) | data formatting | bytes 2097152
